TPU v7x, 32 devices: a whole 2x2x4 slice. The times are simulated.
32 devices in a mesh: group: 2 (over y), slab: 4 (over z), plane: 4 (over x, core).
Axes of the slice: x: 2, y: 2, z: 4, core: 2. Of those that a mesh axis runs over, the one named last changes fastest.
Arguments:
- fields: float32 [2, 32, 128, 1024], P('group', None, 'slab', 'plane'), may hold values from 0 to 2
- evap_rates: float32 [32], replicated, may hold values from 0.05 to 0.5
- coal_kernel: bfloat16 [32, 1024], replicated, may hold values from -0.1875 to 0.1875
- plume_width: float32 [8], replicated, may hold values from 1 to 8
- owner_map: int32 [16, 2048], P(('slab', 'plane')), may hold values from 0 to 15, as said below
- deposit_cell: int32 [16, 2048], P(('slab', 'plane')), may hold values from 0 to 8191
- plume_ids: int32 [16, 2048], P(('slab', 'plane')), may hold values from 0 to 7
Outputs:
- new_fields: float32 [2, 32, 128, 1024], P('group', None, 'slab', 'plane')
Inputs may be any that keep to these rules, and one draw needn't show every extreme that they name: `owner_map`: among the 2048 rows of one index of the first dimension, at most 256 name any one spray block, and one block is named by exactly 256 of them at every index.
All inputs are finite; a program needn't handle non-finite values.
Results may differ from a plain program's by a relative error of at most 0.0014.
Values may be sent and summed in bfloat16 or wider, within the bound.
A program may use at most 64 MiB of HBM per device.

v0:
```python
import functools

import jax
import jax.numpy as jnp
import numpy as np
from jax import lax
from jax.experimental import pallas as pl
from jax.experimental.pallas import tpu as pltpu
from jax.sharding import PartitionSpec as P

MESH = pl.DeviceIdType.MESH
F32 = jnp.float32
BF16 = jnp.bfloat16
LANES = 128
SLOTS = 256
CHUNK = 2
SOURCES = 4

cfl_nozzle = 0.35
diffusion = 0.2
relax_rate = 5.0
relax_step = 0.1
collide_step = 0.25


def fold_matrix(sections):
    kept = [(i, j) for i in range(sections) for j in range(i // 8 * 8, sections)]
    fold = np.zeros((sections * sections, len(kept)), np.float32)
    for q, (i, j) in enumerate(kept):
        fold[i * sections + j, q] = 1.0
        if j // 8 > i // 8:
            fold[j * sections + i, q] = 1.0
    return fold


def pair_terms(m):
    sections, width = m.shape
    pieces = []
    for i in range(sections):
        low = i // 8 * 8
        pieces.append(jnp.broadcast_to(m[i : i + 1], (sections - low, width)) * m[low:])
    return jnp.concatenate(pieces, axis=0).astype(BF16)


def split_hi_lo(x):
    hi = x.astype(BF16)
    lo = (x - hi.astype(F32)).astype(BF16)
    return hi, lo


def dot_last(a, b):
    return lax.dot_general(a, b, (((1,), (1,)), ((), ())), preferred_element_type=F32)


def kernel(
    n_slab, n_plane, sections, ca, cb, exit_rows,
    fields_hbm, evap_ref, coal_ref, fold_hbm, width_ref, owner_ref, cell_ref, pid_ref,
    out_hbm,
    fbuf, tbuf, hbuf, obuf, fold, cols_out, cols_in, par, send_buf, recv_buf,
    in_sem, out_sem, fold_sem, halo_send, halo_recv, row_send, row_recv,
):
    owners = n_slab * n_plane
    plumes = width_ref.shape[0]
    rows = sections * ca
    g = lax.axis_index("group")
    s = lax.axis_index("slab")
    p = lax.axis_index("plane")
    me = s * n_plane + p

    loads = [
        pltpu.make_async_copy(
            fields_hbm.at[0, :, pl.ds(h * LANES, LANES)], fbuf.at[h], in_sem.at[h]
        )
        for h in range(2)
    ]
    for load in loads:
        load.start()
    fold_load = pltpu.make_async_copy(fold_hbm, fold, fold_sem)

    @pl.when(g == 1)
    def _():
        fold_load.start()

    barrier = pltpu.get_barrier_semaphore()
    sides = [
        (s > 0, (g, s - 1, p)),
        (s < n_slab - 1, (g, s + 1, p)),
        (p > 0, (g, s, p - 1)),
        (p < n_plane - 1, (g, s, p + 1)),
    ]
    near = 0
    for there, target in sides:
        near = near + there.astype(jnp.int32)

        @pl.when(there)
        def _():
            pl.semaphore_signal(barrier, inc=1, device_id=target, device_id_type=MESH)

    @pl.when(g == 1)
    def _():
        @pl.loop(0, owners)
        def _(o):
            pl.semaphore_signal(
                barrier, inc=1, device_id=(0, o // n_plane, o % n_plane), device_id_type=MESH
            )

    pl.semaphore_wait(barrier, near + jnp.where(g == 0, owners, 0))

    for load in loads:
        load.wait()

    def gather_row(ref, a):
        return jnp.concatenate(
            [ref[h, pl.ds(a, sections, stride=ca), :] for h in range(2)], axis=1
        )

    for a in (0, ca - 1):
        tbuf[a + 1] = gather_row(fbuf, a)

    lane = lax.broadcasted_iota(jnp.int32, (8, LANES), 1)
    for h, at in ((0, 0), (1, LANES - 1)):
        select = (lane == at).astype(BF16)
        hi, lo = split_hi_lo(fbuf[h])
        cols_out[h] = (dot_last(select, hi) + dot_last(select, lo))[0:1]

    def halo(kind, target):
        source, landing = (
            (tbuf.at[ca], tbuf.at[0]),
            (tbuf.at[1], tbuf.at[ca + 1]),
            (cols_out.at[1], cols_in.at[0]),
            (cols_out.at[0], cols_in.at[1]),
        )[kind]
        return pltpu.make_async_remote_copy(
            src_ref=source,
            dst_ref=landing,
            send_sem=halo_send.at[kind],
            recv_sem=halo_recv.at[kind],
            device_id=target,
            device_id_type=MESH,
        )

    outgoing = (sides[1], sides[0], sides[3], sides[2])
    for kind in range(4):
        there, target = outgoing[kind]

        @pl.when(there)
        def _():
            halo(kind, target).start()

    @pl.loop(1, ca - 1)
    def _(a):
        tbuf[a + 1] = gather_row(fbuf, a)

    for kind, landing in enumerate((tbuf.at[0], tbuf.at[ca + 1], cols_in.at[0], cols_in.at[1])):

        @pl.when(jnp.logical_not(sides[kind][0]))
        def _():
            landing[...] = jnp.zeros(landing.shape, F32)

    def finish_halo():
        for kind in range(4):

            @pl.when(outgoing[kind][0])
            def _():
                halo(kind, outgoing[kind][1]).wait_send()

            @pl.when(sides[kind][0])
            def _():
                halo(kind, outgoing[kind][1]).wait_recv()

        sub = lax.broadcasted_iota(jnp.int32, (16, LANES), 0)
        lanes = lax.broadcasted_iota(jnp.int32, (16, LANES), 1)
        for h, at in ((0, 0), (1, LANES - 1)):
            hi = cols_in[h].astype(BF16).astype(F32)
            lo = cols_in[h] - hi
            stack = jnp.concatenate([hi, lo, jnp.zeros((14, rows), F32)], axis=0)
            place = jnp.logical_and(sub < 2, lanes == at).astype(BF16)
            hbuf[h] = jnp.dot(stack.T.astype(BF16), place, preferred_element_type=F32)

    col_lane = lax.broadcasted_iota(jnp.int32, (sections, cb), 1)
    col_row = lax.broadcasted_iota(jnp.int32, (sections, cb), 0)

    def neighbours(a):
        c = tbuf[a + 1]
        up = tbuf[a]
        left = jnp.where(col_lane == 0, 0.0, pltpu.roll(c, 1, 1))
        right = jnp.where(col_lane == cb - 1, 0.0, pltpu.roll(c, cb - 1, 1))
        lap = up + tbuf[a + 2] + (left + right + gather_row(hbuf, a)) - 4.0 * c
        return c, up, lap

    def scatter_row(a, value):
        for h in range(2):
            obuf[h, pl.ds(a, sections, stride=ca), :] = value[:, h * LANES : (h + 1) * LANES]

    stores = [
        pltpu.make_async_copy(
            obuf.at[h], out_hbm.at[0, :, pl.ds(h * LANES, LANES)], out_sem.at[h]
        )
        for h in range(2)
    ]

    @pl.when(g == 0)
    def _():
        owner = owner_ref[...]
        slots = []
        below = lax.broadcasted_iota(jnp.int32, (256, 256), 0)
        after = lax.broadcasted_iota(jnp.int32, (256, 256), 1)
        upto = (below <= after).astype(BF16)
        names = lax.broadcasted_iota(jnp.int32, (owners, 256), 0)
        carry = jnp.zeros((owners, 1), F32)
        for j in range(exit_rows // 256):
            hit = (owner[:, j * 256 : (j + 1) * 256] == names).astype(F32)
            count = jnp.dot(hit.astype(BF16), upto, preferred_element_type=F32) + carry
            slots.append(jnp.sum(hit * (count - 1.0), axis=0, keepdims=True))
            carry = count[:, 255:256]
        slot = jnp.concatenate(slots, axis=1)
        cell = cell_ref[...]
        across = jnp.bitwise_and(cell, cb - 1)
        along = jnp.right_shift(cell, cb.bit_length() - 1)
        par[4:5] = pid_ref[...].astype(F32)
        par[5:6] = along.astype(F32)
        par[6:7] = across.astype(F32)
        par[7:8] = jnp.zeros((1, exit_rows), F32)
        places = lax.broadcasted_iota(jnp.int32, (SLOTS, exit_rows), 0).astype(F32)
        in_slot = (slot == places).astype(BF16)

        finish_halo()

        @pl.loop(0, ca)
        def _(a):
            c, _, lap = neighbours(a)
            back = jnp.where(jnp.bitwise_and(col_row, 7) == 0, 0.0, pltpu.roll(c, 1, 0))
            du = c - back
            layers = sections // 4
            d, m, q, e = (c[v * layers : (v + 1) * layers] for v in range(4))
            dm, dq, de = (du[v * layers : (v + 1) * layers] for v in (1, 2, 3))
            relaxing = relax_rate / (1.0 + d * d)
            fresh = diffusion * lap + jnp.concatenate(
                [
                    d - cfl_nozzle * dm,
                    m - cfl_nozzle * (dm + dq),
                    q + relax_step * relaxing * (e - q) - cfl_nozzle * dq,
                    e - cfl_nozzle * de,
                ],
                axis=0,
            )
            scatter_row(a, fresh)

        for store in stores:
            store.start()

        layers = sections // 4
        halve = jnp.where(
            jnp.right_shift(lax.broadcasted_iota(jnp.int32, (cb, cb // 2), 0), 1)
            == lax.broadcasted_iota(jnp.int32, (cb, cb // 2), 1),
            0.5,
            0.0,
        ).astype(F32)
        halve_rows = jnp.where(
            jnp.right_shift(lax.broadcasted_iota(jnp.int32, (ca // 2, ca), 1), 1)
            == lax.broadcasted_iota(jnp.int32, (ca // 2, ca), 0),
            0.5,
            0.0,
        ).astype(F32)
        coarse = []
        for v in (1, 2, 3):
            at = pl.ds((v * layers + layers - 1) * ca, ca)
            plane = jnp.concatenate([obuf[h, at, :] for h in range(2)], axis=1)
            half = jnp.dot(
                plane, halve, precision=lax.Precision.HIGHEST, preferred_element_type=F32
            )
            coarse.append(
                jnp.dot(
                    halve_rows, half, precision=lax.Precision.HIGHEST, preferred_element_type=F32
                )
            )
        flux, quality, enthalpy = coarse
        strength = jnp.sqrt(1.0 + flux * flux)
        center = (sections - 1) * jax.nn.sigmoid(enthalpy - 2.0 * quality)
        for base, value in ((0, strength), (2, center)):
            hi, lo = split_hi_lo(value)
            for k, part in ((base, hi.astype(F32)), (base + 1, lo.astype(F32))):
                for i in range(ca // 2):
                    par[k : k + 1, i * (cb // 2) : (i + 1) * (cb // 2)] = part[i : i + 1]

        group = 16
        values = par[...]
        tiled = jnp.concatenate([values] * group, axis=0)
        label = jnp.right_shift(lax.broadcasted_iota(jnp.int32, (group * 8, exit_rows), 0), 3)

        @pl.loop(0, owners // group)
        def _(b):
            picked = jnp.where(owner == label + b * group, tiled, 0.0).astype(BF16)
            packed = dot_last(picked, in_slot).reshape(group, 8, SLOTS)
            send_buf[pl.ds(b * group, group)] = jnp.concatenate(
                [packed[:, :, :LANES], packed[:, :, LANES:]], axis=1
            ).astype(BF16)

            @pl.loop(0, group)
            def _(k):
                o = b * group + k
                pltpu.make_async_remote_copy(
                    src_ref=send_buf.at[o],
                    dst_ref=recv_buf.at[me],
                    send_sem=row_send.at[o],
                    recv_sem=row_recv.at[me],
                    device_id=(1, o // n_plane, o % n_plane),
                    device_id_type=MESH,
                ).start()

        @pl.loop(0, owners)
        def _(o):
            pltpu.make_async_remote_copy(
                src_ref=send_buf.at[o],
                dst_ref=recv_buf.at[me],
                send_sem=row_send.at[o],
                recv_sem=row_recv.at[me],
                device_id=(1, o // n_plane, o % n_plane),
                device_id_type=MESH,
            ).wait_send()

    @pl.when(g == 1)
    def _():
        fold_load.wait()
        folded = jnp.dot(coal_ref[...], fold[...], preferred_element_type=F32).astype(BF16)
        evap = jnp.zeros((sections, cb), F32)
        for k in range(sections):
            evap = jnp.where(col_row == k, evap_ref[k], evap)
        speeds = 0.2 + 0.5 * col_row.astype(F32) / (sections - 1)

        finish_halo()

        @pl.loop(0, ca // CHUNK)
        def _(step):
            parts = []
            for t in range(CHUNK):
                c, up, lap = neighbours(step * CHUNK + t)
                lost = evap * c
                gained = jnp.where(
                    col_row == sections - 1, 0.0, pltpu.roll(lost, sections - 1, 0)
                )
                parts.append(c - speeds * (c - up) + diffusion * lap - lost + gained)
            moved = jnp.concatenate(parts, axis=1)
            first = jnp.dot(folded, pair_terms(moved), preferred_element_type=F32)
            middle = moved + (0.5 * collide_step) * first
            second = jnp.dot(folded, pair_terms(middle), preferred_element_type=F32)
            mixed = moved + collide_step * second
            for t in range(CHUNK):
                scatter_row(step * CHUNK + t, mixed[:, t * cb : (t + 1) * cb])

        level = lax.broadcasted_iota(jnp.int32, (sections, SLOTS), 0).astype(F32)
        index_a = lax.broadcasted_iota(jnp.int32, (ca, SLOTS), 0).astype(F32)
        index_b = lax.broadcasted_iota(jnp.int32, (cb, SLOTS), 0).astype(F32)

        @pl.loop(0, owners // SOURCES)
        def _(step):
            lefts, rights = [], []
            for t in range(SOURCES):
                o = step * SOURCES + t
                pltpu.make_async_remote_copy(
                    src_ref=send_buf.at[o],
                    dst_ref=recv_buf.at[o],
                    send_sem=row_send.at[o],
                    recv_sem=row_recv.at[o],
                    device_id=(0, s, p),
                    device_id_type=MESH,
                ).wait_recv()
                block = recv_buf[o].astype(F32)
                got = jnp.concatenate([block[:8], block[8:]], axis=1)
                strength = got[0:1] + got[1:2]
                center = got[2:3] + got[3:4]
                spread = jnp.full((1, SLOTS), width_ref[0], F32)
                for k in range(1, plumes):
                    spread = jnp.where(got[4:5] == float(k), width_ref[k], spread)
                scaled = (level - center) / spread
                weights = 1.0 / (1.0 + scaled * scaled)
                masses = strength * weights / jnp.sum(weights, axis=0, keepdims=True)
                mask = (got[5:6] == index_a).astype(BF16)
                lefts.append(
                    jnp.concatenate(
                        [
                            jnp.broadcast_to(masses[k : k + 1], (ca, SLOTS)).astype(BF16) * mask
                            for k in range(sections)
                        ],
                        axis=0,
                    )
                )
                rights.append((got[6:7] == index_b).astype(BF16))
            left = jnp.concatenate(lefts, axis=1)
            right = jnp.concatenate(rights, axis=1)
            added = dot_last(left, right)
            for h in range(2):
                obuf[h] += added[:, h * LANES : (h + 1) * LANES]

        for store in stores:
            store.start()

    for store in stores:
        store.wait()


def body(n_slab, n_plane, fields, evap_rates, coal_kernel, plume_width, owner_map, deposit_cell, plume_ids):
    _, sections, ca, cb = fields.shape
    exit_rows = owner_map.shape[1]
    owners = n_slab * n_plane
    rows = sections * ca
    fold = jnp.asarray(fold_matrix(sections), BF16)
    kept = fold.shape[1]
    hbm = pl.BlockSpec(memory_space=pl.ANY)
    vmem = pl.BlockSpec(memory_space=pltpu.VMEM)
    smem = pl.BlockSpec(memory_space=pltpu.SMEM)
    out = pl.pallas_call(
        functools.partial(kernel, n_slab, n_plane, sections, ca, cb, exit_rows),
        out_shape=jax.ShapeDtypeStruct((1, rows, cb), F32),
        in_specs=[hbm, smem, vmem, hbm, smem, vmem, vmem, vmem],
        out_specs=hbm,
        scratch_shapes=[
            pltpu.VMEM((2, rows, LANES), F32),
            pltpu.VMEM((ca + 2, sections, cb), F32),
            pltpu.VMEM((2, rows, LANES), F32),
            pltpu.VMEM((2, rows, LANES), F32),
            pltpu.VMEM((sections * sections, kept), BF16),
            pltpu.VMEM((2, 1, rows), F32),
            pltpu.VMEM((2, 1, rows), F32),
            pltpu.VMEM((8, exit_rows), F32),
            pltpu.VMEM((owners, 16, LANES), BF16),
            pltpu.VMEM((owners, 16, LANES), BF16),
            pltpu.SemaphoreType.DMA((2,)),
            pltpu.SemaphoreType.DMA((2,)),
            pltpu.SemaphoreType.DMA,
            pltpu.SemaphoreType.DMA((4,)),
            pltpu.SemaphoreType.DMA((4,)),
            pltpu.SemaphoreType.DMA((owners,)),
            pltpu.SemaphoreType.DMA((owners,)),
        ],
        compiler_params=pltpu.CompilerParams(
            collective_id=0, has_side_effects=True, vmem_limit_bytes=48 * 1024 * 1024
        ),
    )(
        fields.reshape(1, rows, cb), evap_rates, coal_kernel, fold, plume_width,
        owner_map, deposit_cell, plume_ids,
    )
    return out.reshape(1, sections, ca, cb)


def solution(mesh):
    return jax.shard_map(
        functools.partial(body, mesh.shape["slab"], mesh.shape["plane"]),
        mesh=mesh,
        in_specs=(
            P("group", None, "slab", "plane"),
            P(),
            P(),
            P(),
            P(("slab", "plane"), None),
            P(("slab", "plane"), None),
            P(("slab", "plane"), None),
        ),
        out_specs=P("group", None, "slab", "plane"),
        check_vma=False,
    )
```

profile of v0, /device:TPU:7, one launch (start us, length us, event | category | flops | bytes accessed | tf_op | source)
XLA Modules:
  0.0 29.4 jit_solution(11027145429006343480)
XLA Ops:
  0.0 0.0 copy-start
  0.0 1.3 %copy-done = bf16[1024,640]{1,0:T(8,128)(2,1)S(1)} copy-done((bf16[1024,640]{1,0:T(8,128)(2,1)S(1)}, bf16[1024,640]{1,0:T(8,128)(2,1)}, u32[]{:S(2)}) %copy-start) | copy-done | bytes 1310744
  1.3 0.0 copy-start.1
  1.3 1.2 %copy-done.1 = f32[1,32,32,256]{3,2,1,0:T(8,128)S(1)} copy-done((f32[1,32,32,256]{3,2,1,0:T(8,128)S(1)}, f32[1,32,32,256]{3,2,1,0:T(8,128)}, u32[]{:S(2)}) %copy-start.1) | copy-done | bytes 1048600
  2.5 0.0 copy-start.2
  2.5 0.8 %copy-done.2 = bf16[32,1024]{1,0:T(8,128)(2,1)S(1)} copy-done((bf16[32,1024]{1,0:T(8,128)(2,1)S(1)}, bf16[32,1024]{1,0:T(8,128)(2,1)}, u32[]{:S(2)}) %copy-start.2) | copy-done | bytes 65560
  3.4 0.0 copy-start.3
  3.4 0.7 %copy-done.3 = s32[1,2048]{1,0:T(1,128)S(1)} copy-done((s32[1,2048]{1,0:T(1,128)S(1)}, s32[1,2048]{1,0:T(1,128)}, u32[]{:S(2)}) %copy-start.3) | copy-done | bytes 8216
  4.1 0.0 copy-start.4
  4.1 0.7 %copy-done.4 = s32[1,2048]{1,0:T(1,128)S(1)} copy-done((s32[1,2048]{1,0:T(1,128)S(1)}, s32[1,2048]{1,0:T(1,128)}, u32[]{:S(2)}) %copy-start.4) | copy-done | bytes 8216
  4.8 0.0 copy-start.5
  4.8 0.7 %copy-done.5 = s32[1,2048]{1,0:T(1,128)S(1)} copy-done((s32[1,2048]{1,0:T(1,128)S(1)}, s32[1,2048]{1,0:T(1,128)}, u32[]{:S(2)}) %copy-start.5) | copy-done | bytes 8216
  5.5 0.0 copy-start.6
  5.5 0.7 %copy-done.6 = f32[32]{0:T(128)S(1)} copy-done((f32[32]{0:T(128)S(1)}, f32[32]{0:T(128)}, u32[]{:S(2)}) %copy-start.6) | copy-done | bytes 152
  6.1 0.0 copy-start.7
  6.1 0.7 %copy-done.7 = f32[8]{0:T(128)S(1)} copy-done((f32[8]{0:T(128)S(1)}, f32[8]{0:T(128)}, u32[]{:S(2)}) %copy-start.7) | copy-done | bytes 56
  6.8 21.7 %shard_map.82 = f32[1,1024,256]{2,1,0:T(8,128)S(1)} custom-call(f32[1,1024,256]{2,1,0:T(8,128)S(1)} %bitcast.3, f32[32]{0:T(128)S(1)} %copy-done.6, bf16[32,1024]{1,0:T(8,128)(2,1)S(1)} %copy-done.2, bf16[1024,640]{1,0:T(8,128)(2,1)S(1)} %copy-done, f32[8]{0:T(128)S(1)} %copy-done.7, s32[1,2048]{1,0:T(1,128)S(1)} %copy-done.3, s32[1,2048]{1,0:T(1,128)S(1)} %copy-done.4, ...), custom_call_target="tpu_custom_call" | custom-call | tf_op jit(solution)/shard_map/pallas_call | solution.py:412
  28.5 1.0 %copy.10 = f32[1,32,32,256]{3,2,1,0:T(8,128)} copy(f32[1,32,32,256]{3,2,1,0:T(8,128)S(1)} %bitcast.2) | data formatting | bytes 2097152
Async XLA Ops:
  0.0 1.3 %copy-start = (bf16[1024,640]{1,0:T(8,128)(2,1)S(1)}, bf16[1024,640]{1,0:T(8,128)(2,1)}, u32[]{:S(2)}) copy-start(bf16[1024,640]{1,0:T(8,128)(2,1)} %constant.2.clone.fold_hbm) | copy-start | bytes 3932164
  1.3 1.2 %copy-start.1 = (f32[1,32,32,256]{3,2,1,0:T(8,128)S(1)}, f32[1,32,32,256]{3,2,1,0:T(8,128)}, u32[]{:S(2)}) copy-start(f32[1,32,32,256]{3,2,1,0:T(8,128)} %param.8) | copy-start | bytes 3145732
  2.5 0.8 %copy-start.2 = (bf16[32,1024]{1,0:T(8,128)(2,1)S(1)}, bf16[32,1024]{1,0:T(8,128)(2,1)}, u32[]{:S(2)}) copy-start(bf16[32,1024]{1,0:T(8,128)(2,1)} %coal_ref.1) | copy-start | bytes 196612
  3.4 0.7 %copy-start.3 = (s32[1,2048]{1,0:T(1,128)S(1)}, s32[1,2048]{1,0:T(1,128)}, u32[]{:S(2)}) copy-start(s32[1,2048]{1,0:T(1,128)} %owner_ref.1) | copy-start | bytes 24580
  4.1 0.7 %copy-start.4 = (s32[1,2048]{1,0:T(1,128)S(1)}, s32[1,2048]{1,0:T(1,128)}, u32[]{:S(2)}) copy-start(s32[1,2048]{1,0:T(1,128)} %cell_ref.1) | copy-start | bytes 24580
  4.8 0.7 %copy-start.5 = (s32[1,2048]{1,0:T(1,128)S(1)}, s32[1,2048]{1,0:T(1,128)}, u32[]{:S(2)}) copy-start(s32[1,2048]{1,0:T(1,128)} %pid_ref.1) | copy-start | bytes 24580
  5.5 0.7 %copy-start.6 = (f32[32]{0:T(128)S(1)}, f32[32]{0:T(128)}, u32[]{:S(2)}) copy-start(f32[32]{0:T(128)} %evap_ref.1) | copy-start | bytes 388
  6.1 0.7 %copy-start.7 = (f32[8]{0:T(128)S(1)}, f32[8]{0:T(128)}, u32[]{:S(2)}) copy-start(f32[8]{0:T(128)} %width_ref.1) | copy-start | bytes 100
where the time goes:
time: 29.9 us; the launch traced here: 29.4 us
  Pallas kernels  21.7 us (73%)
  local copies, waits for them, and re-layouts  7.75 us (26%)
    pallas_call x1, Pallas kernels, body(): pl.pallas_call(functools.partial(kernel, n_slab, n_plane, sections, ca, c...  21.7 us
    unnamed x17, local copies, waits for them, and re-layouts  7.75 us

commit v1 on v0

--- a/solution.py
+++ b/solution.py
@@ -15,6 +15,7 @@
 SLOTS = 256
 CHUNK = 2
 SOURCES = 4
+VMEM_BYTES = 63 * 1024 * 1024
 
 cfl_nozzle = 0.35
 diffusion = 0.2
@@ -54,10 +55,11 @@
 
 def kernel(
     n_slab, n_plane, sections, ca, cb, exit_rows,
-    fields_hbm, evap_ref, coal_ref, fold_hbm, width_ref, owner_ref, cell_ref, pid_ref,
+    fields_hbm, evap_hbm, coal_hbm, fold_hbm, width_hbm, owner_hbm, cell_hbm, pid_hbm,
     out_hbm,
     fbuf, tbuf, hbuf, obuf, fold, cols_out, cols_in, par, send_buf, recv_buf,
-    in_sem, out_sem, fold_sem, halo_send, halo_recv, row_send, row_recv,
+    evap_ref, coal_ref, width_ref, owner_ref, cell_ref, pid_ref,
+    in_sem, out_sem, arg_sem, halo_send, halo_recv, row_send, row_recv,
 ):
     owners = n_slab * n_plane
     plumes = width_ref.shape[0]
@@ -66,20 +68,6 @@
     s = lax.axis_index("slab")
     p = lax.axis_index("plane")
     me = s * n_plane + p
-
-    loads = [
-        pltpu.make_async_copy(
-            fields_hbm.at[0, :, pl.ds(h * LANES, LANES)], fbuf.at[h], in_sem.at[h]
-        )
-        for h in range(2)
-    ]
-    for load in loads:
-        load.start()
-    fold_load = pltpu.make_async_copy(fold_hbm, fold, fold_sem)
-
-    @pl.when(g == 1)
-    def _():
-        fold_load.start()
 
     barrier = pltpu.get_barrier_semaphore()
     sides = [
@@ -104,15 +92,41 @@
                 barrier, inc=1, device_id=(0, o // n_plane, o % n_plane), device_id_type=MESH
             )
 
-    pl.semaphore_wait(barrier, near + jnp.where(g == 0, owners, 0))
-
-    for load in loads:
-        load.wait()
+    load = pltpu.make_async_copy(fields_hbm, fbuf, in_sem)
+    load.start()
+    nozzle_args = [
+        pltpu.make_async_copy(source, target, arg_sem.at[k])
+        for k, (source, target) in enumerate(
+            ((owner_hbm, owner_ref), (cell_hbm, cell_ref), (pid_hbm, pid_ref))
+        )
+    ]
+    spray_args = [
+        pltpu.make_async_copy(source, target, arg_sem.at[k])
+        for k, (source, target) in enumerate(
+            ((evap_hbm, evap_ref), (width_hbm, width_ref), (coal_hbm, coal_ref), (fold_hbm, fold))
+        )
+    ]
+
+    @pl.when(g == 0)
+    def _():
+        for copy in nozzle_args:
+            copy.start()
+
+    @pl.when(g == 1)
+    def _():
+        for copy in spray_args:
+            copy.start()
+
+    load.wait()
+
+    def lines(a, h):
+        return pl.ds(a // 8 * 16 + h * 8 + a % 8, sections, stride=2 * ca)
 
     def gather_row(ref, a):
-        return jnp.concatenate(
-            [ref[h, pl.ds(a, sections, stride=ca), :] for h in range(2)], axis=1
-        )
+        return jnp.concatenate([ref[lines(a, h), :] for h in range(2)], axis=1)
+
+    def half(ref, h):
+        return ref[...].reshape(rows // 8, 2, 8, LANES)[:, h].reshape(rows, LANES)
 
     for a in (0, ca - 1):
         tbuf[a + 1] = gather_row(fbuf, a)
@@ -120,7 +134,7 @@
     lane = lax.broadcasted_iota(jnp.int32, (8, LANES), 1)
     for h, at in ((0, 0), (1, LANES - 1)):
         select = (lane == at).astype(BF16)
-        hi, lo = split_hi_lo(fbuf[h])
+        hi, lo = split_hi_lo(half(fbuf, h))
         cols_out[h] = (dot_last(select, hi) + dot_last(select, lo))[0:1]
 
     def halo(kind, target):
@@ -139,6 +153,8 @@
             device_id_type=MESH,
         )
 
+    pl.semaphore_wait(barrier, near + jnp.where(g == 0, owners, 0))
+
     outgoing = (sides[1], sides[0], sides[3], sides[2])
     for kind in range(4):
         there, target = outgoing[kind]
@@ -175,32 +191,35 @@
             lo = cols_in[h] - hi
             stack = jnp.concatenate([hi, lo, jnp.zeros((14, rows), F32)], axis=0)
             place = jnp.logical_and(sub < 2, lanes == at).astype(BF16)
-            hbuf[h] = jnp.dot(stack.T.astype(BF16), place, preferred_element_type=F32)
+            placed = jnp.dot(stack.T.astype(BF16), place, preferred_element_type=F32)
+            hbuf[h] = placed
 
     col_lane = lax.broadcasted_iota(jnp.int32, (sections, cb), 1)
     col_row = lax.broadcasted_iota(jnp.int32, (sections, cb), 0)
+
+    def column_halo(a):
+        return jnp.concatenate(
+            [hbuf[h, pl.ds(a, sections, stride=ca), :] for h in range(2)], axis=1
+        )
 
     def neighbours(a):
         c = tbuf[a + 1]
         up = tbuf[a]
         left = jnp.where(col_lane == 0, 0.0, pltpu.roll(c, 1, 1))
         right = jnp.where(col_lane == cb - 1, 0.0, pltpu.roll(c, cb - 1, 1))
-        lap = up + tbuf[a + 2] + (left + right + gather_row(hbuf, a)) - 4.0 * c
+        lap = up + tbuf[a + 2] + (left + right + column_halo(a)) - 4.0 * c
         return c, up, lap
 
     def scatter_row(a, value):
         for h in range(2):
-            obuf[h, pl.ds(a, sections, stride=ca), :] = value[:, h * LANES : (h + 1) * LANES]
-
-    stores = [
-        pltpu.make_async_copy(
-            obuf.at[h], out_hbm.at[0, :, pl.ds(h * LANES, LANES)], out_sem.at[h]
-        )
-        for h in range(2)
-    ]
+            obuf[lines(a, h), :] = value[:, h * LANES : (h + 1) * LANES]
+
+    store = pltpu.make_async_copy(obuf, out_hbm, out_sem)
 
     @pl.when(g == 0)
     def _():
+        for copy in nozzle_args:
+            copy.wait()
         owner = owner_ref[...]
         slots = []
         below = lax.broadcasted_iota(jnp.int32, (256, 256), 0)
@@ -246,8 +265,7 @@
             )
             scatter_row(a, fresh)
 
-        for store in stores:
-            store.start()
+        store.start()
 
         layers = sections // 4
         halve = jnp.where(
@@ -264,14 +282,15 @@
         ).astype(F32)
         coarse = []
         for v in (1, 2, 3):
-            at = pl.ds((v * layers + layers - 1) * ca, ca)
-            plane = jnp.concatenate([obuf[h, at, :] for h in range(2)], axis=1)
-            half = jnp.dot(
+            at = pl.ds((v * layers + layers - 1) * 2 * ca, 2 * ca)
+            tiles = obuf[at, :].reshape(ca // 8, 2, 8, LANES)
+            plane = jnp.concatenate([tiles[:, h].reshape(ca, LANES) for h in range(2)], axis=1)
+            across_mean = jnp.dot(
                 plane, halve, precision=lax.Precision.HIGHEST, preferred_element_type=F32
             )
             coarse.append(
                 jnp.dot(
-                    halve_rows, half, precision=lax.Precision.HIGHEST, preferred_element_type=F32
+                    halve_rows, across_mean, precision=lax.Precision.HIGHEST, preferred_element_type=F32
                 )
             )
         flux, quality, enthalpy = coarse
@@ -321,7 +340,8 @@
 
     @pl.when(g == 1)
     def _():
-        fold_load.wait()
+        for copy in spray_args:
+            copy.wait()
         folded = jnp.dot(coal_ref[...], fold[...], preferred_element_type=F32).astype(BF16)
         evap = jnp.zeros((sections, cb), F32)
         for k in range(sections):
@@ -389,14 +409,15 @@
             left = jnp.concatenate(lefts, axis=1)
             right = jnp.concatenate(rights, axis=1)
             added = dot_last(left, right)
-            for h in range(2):
-                obuf[h] += added[:, h * LANES : (h + 1) * LANES]
-
-        for store in stores:
-            store.start()
-
-    for store in stores:
-        store.wait()
+            tiles = jnp.stack(
+                [added[:, h * LANES : (h + 1) * LANES].reshape(rows // 8, 8, LANES) for h in range(2)],
+                axis=1,
+            )
+            obuf[...] += tiles.reshape(2 * rows, LANES)
+
+        store.start()
+
+    store.wait()
 
 
 def body(n_slab, n_plane, fields, evap_rates, coal_kernel, plume_width, owner_map, deposit_cell, plume_ids):
@@ -407,39 +428,44 @@
     fold = jnp.asarray(fold_matrix(sections), BF16)
     kept = fold.shape[1]
     hbm = pl.BlockSpec(memory_space=pl.ANY)
-    vmem = pl.BlockSpec(memory_space=pltpu.VMEM)
-    smem = pl.BlockSpec(memory_space=pltpu.SMEM)
     out = pl.pallas_call(
         functools.partial(kernel, n_slab, n_plane, sections, ca, cb, exit_rows),
-        out_shape=jax.ShapeDtypeStruct((1, rows, cb), F32),
-        in_specs=[hbm, smem, vmem, hbm, smem, vmem, vmem, vmem],
+        out_shape=jax.ShapeDtypeStruct((2 * rows, LANES), F32),
+        in_specs=[hbm] * 8,
         out_specs=hbm,
         scratch_shapes=[
-            pltpu.VMEM((2, rows, LANES), F32),
+            pltpu.VMEM((2 * rows, LANES), F32),
             pltpu.VMEM((ca + 2, sections, cb), F32),
             pltpu.VMEM((2, rows, LANES), F32),
-            pltpu.VMEM((2, rows, LANES), F32),
+            pltpu.VMEM((2 * rows, LANES), F32),
             pltpu.VMEM((sections * sections, kept), BF16),
             pltpu.VMEM((2, 1, rows), F32),
             pltpu.VMEM((2, 1, rows), F32),
             pltpu.VMEM((8, exit_rows), F32),
             pltpu.VMEM((owners, 16, LANES), BF16),
             pltpu.VMEM((owners, 16, LANES), BF16),
-            pltpu.SemaphoreType.DMA((2,)),
-            pltpu.SemaphoreType.DMA((2,)),
+            pltpu.SMEM(evap_rates.shape, F32),
+            pltpu.VMEM(coal_kernel.shape, BF16),
+            pltpu.SMEM(plume_width.shape, F32),
+            pltpu.VMEM((1, exit_rows), jnp.int32),
+            pltpu.VMEM((1, exit_rows), jnp.int32),
+            pltpu.VMEM((1, exit_rows), jnp.int32),
             pltpu.SemaphoreType.DMA,
+            pltpu.SemaphoreType.DMA,
+            pltpu.SemaphoreType.DMA((4,)),
             pltpu.SemaphoreType.DMA((4,)),
             pltpu.SemaphoreType.DMA((4,)),
             pltpu.SemaphoreType.DMA((owners,)),
             pltpu.SemaphoreType.DMA((owners,)),
         ],
         compiler_params=pltpu.CompilerParams(
-            collective_id=0, has_side_effects=True, vmem_limit_bytes=48 * 1024 * 1024
+            collective_id=0, has_side_effects=True, vmem_limit_bytes=VMEM_BYTES
         ),
     )(
-        fields.reshape(1, rows, cb), evap_rates, coal_kernel, fold, plume_width,
+        fields.reshape(rows // 8, 8, 2, LANES).transpose(0, 2, 1, 3).reshape(2 * rows, LANES), evap_rates, coal_kernel, fold, plume_width,
         owner_map, deposit_cell, plume_ids,
     )
+    out = out.reshape(rows // 8, 2, 8, LANES).transpose(0, 2, 1, 3)
     return out.reshape(1, sections, ca, cb)
 
 

time: 29.9 us -> 23.6 us (0.79); the launches traced: 29.4 us -> 23.4 us
  local copies, waits for them, and re-layouts: 7.75 us -> 2.31 us
  Pallas kernels: 21.7 us -> 21.1 us
    unnamed x17 -> x1, local copies, waits for them, and re-layouts: 7.75 us -> 2.31 us
    pallas_call x1, Pallas kernels: 21.7 us -> 21.1 us  [body(): pl.pallas_call(functools.partial(kernel, n_slab, n_plane, sections, ca, c...]
where the time goes in v1:
time: 23.6 us; the launch traced here: 23.4 us
  Pallas kernels  21.1 us (89%)
  local copies, waits for them, and re-layouts  2.31 us (10%)
    pallas_call x1, Pallas kernels, body(): pl.pallas_call(functools.partial(kernel, n_slab, n_plane, sections, ca, c...  21.1 us
    unnamed x1, local copies, waits for them, and re-layouts  2.31 us

profile of v1, /device:TPU:7, one launch (start us, length us, event | category | flops | bytes accessed | tf_op | source)
XLA Modules:
  0.0 23.4 jit_solution(1993012156118962646)
XLA Ops:
  0.0 21.1 %shard_map.82 = f32[2048,128]{1,0:T(8,128)} custom-call(f32[2048,128]{1,0:T(8,128)} %bitcast.11, f32[32]{0:T(128)} %evap_hbm.1, bf16[32,1024]{1,0:T(8,128)(2,1)} %coal_hbm.1, bf16[1024,640]{1,0:T(8,128)(2,1)} %constant.2.clone.fold_hbm, f32[8]{0:T(128)} %width_hbm.1, s32[1,2048]{1,0:T(1,128)} %owner_hbm.1, s32[1,2048]{1,0:T(1,128)} %cell_hbm.1, ...), custom_call_target="tpu_custom_call" | custom-call | tf_op jit(solution)/shard_map/pallas_call | solution.py:431
  21.1 2.3 %copy.10 = f32[1,32,32,256]{3,2,1,0:T(8,128)} copy(f32[1,32,32,256]{3,2,1,0:T(8,128)} %bitcast.10) | data formatting | bytes 2097152

commit v2 on v1

--- a/solution.py
+++ b/solution.py
@@ -13,7 +13,7 @@
 BF16 = jnp.bfloat16
 LANES = 128
 SLOTS = 256
-CHUNK = 2
+CHUNK = 4
 SOURCES = 4
 VMEM_BYTES = 63 * 1024 * 1024
 
@@ -58,7 +58,7 @@
     fields_hbm, evap_hbm, coal_hbm, fold_hbm, width_hbm, owner_hbm, cell_hbm, pid_hbm,
     out_hbm,
     fbuf, tbuf, hbuf, obuf, fold, cols_out, cols_in, par, send_buf, recv_buf,
-    evap_ref, coal_ref, width_ref, owner_ref, cell_ref, pid_ref,
+    evap_ref, coal_ref, width_ref, owner_ref, cell_ref, pid_ref, picks, in_slot,
     in_sem, out_sem, arg_sem, halo_send, halo_recv, row_send, row_recv,
 ):
     owners = n_slab * n_plane
@@ -130,12 +130,6 @@
 
     for a in (0, ca - 1):
         tbuf[a + 1] = gather_row(fbuf, a)
-
-    lane = lax.broadcasted_iota(jnp.int32, (8, LANES), 1)
-    for h, at in ((0, 0), (1, LANES - 1)):
-        select = (lane == at).astype(BF16)
-        hi, lo = split_hi_lo(half(fbuf, h))
-        cols_out[h] = (dot_last(select, hi) + dot_last(select, lo))[0:1]
 
     def halo(kind, target):
         source, landing = (
@@ -156,12 +150,21 @@
     pl.semaphore_wait(barrier, near + jnp.where(g == 0, owners, 0))
 
     outgoing = (sides[1], sides[0], sides[3], sides[2])
-    for kind in range(4):
-        there, target = outgoing[kind]
-
-        @pl.when(there)
-        def _():
-            halo(kind, target).start()
+    def start_halo(kinds):
+        for kind in kinds:
+
+            @pl.when(outgoing[kind][0])
+            def _():
+                halo(kind, outgoing[kind][1]).start()
+
+    start_halo((0, 1))
+
+    lane = lax.broadcasted_iota(jnp.int32, (8, LANES), 1)
+    for h, at in ((0, 0), (1, LANES - 1)):
+        select = (lane == at).astype(BF16)
+        cols_out[h] = dot_last(select, half(fbuf, h).astype(BF16))[0:1]
+
+    start_halo((2, 3))
 
     @pl.loop(1, ca - 1)
     def _(a):
@@ -184,15 +187,15 @@
             def _():
                 halo(kind, outgoing[kind][1]).wait_recv()
 
-        sub = lax.broadcasted_iota(jnp.int32, (16, LANES), 0)
-        lanes = lax.broadcasted_iota(jnp.int32, (16, LANES), 1)
-        for h, at in ((0, 0), (1, LANES - 1)):
-            hi = cols_in[h].astype(BF16).astype(F32)
-            lo = cols_in[h] - hi
-            stack = jnp.concatenate([hi, lo, jnp.zeros((14, rows), F32)], axis=0)
-            place = jnp.logical_and(sub < 2, lanes == at).astype(BF16)
-            placed = jnp.dot(stack.T.astype(BF16), place, preferred_element_type=F32)
-            hbuf[h] = placed
+        sub = lax.broadcasted_iota(jnp.int32, (16, cb), 0)
+        lanes = lax.broadcasted_iota(jnp.int32, (16, cb), 1)
+        stack = jnp.concatenate([cols_in[0], cols_in[1], jnp.zeros((14, rows), F32)], axis=0)
+        place = jnp.logical_or(
+            jnp.logical_and(sub == 0, lanes == 0), jnp.logical_and(sub == 1, lanes == cb - 1)
+        ).astype(BF16)
+        placed = jnp.dot(stack.T.astype(BF16), place, preferred_element_type=F32)
+        for h in range(2):
+            hbuf[h] = placed[:, h * LANES : (h + 1) * LANES]
 
     col_lane = lax.broadcasted_iota(jnp.int32, (sections, cb), 1)
     col_row = lax.broadcasted_iota(jnp.int32, (sections, cb), 0)
@@ -241,76 +244,83 @@
         par[6:7] = across.astype(F32)
         par[7:8] = jnp.zeros((1, exit_rows), F32)
         places = lax.broadcasted_iota(jnp.int32, (SLOTS, exit_rows), 0).astype(F32)
-        in_slot = (slot == places).astype(BF16)
-
-        finish_halo()
-
-        @pl.loop(0, ca)
-        def _(a):
-            c, _, lap = neighbours(a)
-            back = jnp.where(jnp.bitwise_and(col_row, 7) == 0, 0.0, pltpu.roll(c, 1, 0))
-            du = c - back
-            layers = sections // 4
-            d, m, q, e = (c[v * layers : (v + 1) * layers] for v in range(4))
-            dm, dq, de = (du[v * layers : (v + 1) * layers] for v in (1, 2, 3))
-            relaxing = relax_rate / (1.0 + d * d)
-            fresh = diffusion * lap + jnp.concatenate(
-                [
-                    d - cfl_nozzle * dm,
-                    m - cfl_nozzle * (dm + dq),
-                    q + relax_step * relaxing * (e - q) - cfl_nozzle * dq,
-                    e - cfl_nozzle * de,
-                ],
-                axis=0,
-            )
-            scatter_row(a, fresh)
-
-        store.start()
-
-        layers = sections // 4
+        in_slot[...] = (slot == places).astype(BF16)
+        group = 16
+        label = jnp.right_shift(lax.broadcasted_iota(jnp.int32, (group * 8, exit_rows), 0), 3)
+
+        @pl.loop(0, owners // group)
+        def _(b):
+            picks[pl.ds(pl.multiple_of(b * group * 8, group * 8), group * 8)] = (
+                owner == label + b * group
+            ).astype(BF16)
+
         halve = jnp.where(
             jnp.right_shift(lax.broadcasted_iota(jnp.int32, (cb, cb // 2), 0), 1)
             == lax.broadcasted_iota(jnp.int32, (cb, cb // 2), 1),
-            0.5,
+            0.25,
             0.0,
-        ).astype(F32)
-        halve_rows = jnp.where(
-            jnp.right_shift(lax.broadcasted_iota(jnp.int32, (ca // 2, ca), 1), 1)
-            == lax.broadcasted_iota(jnp.int32, (ca // 2, ca), 0),
-            0.5,
-            0.0,
-        ).astype(F32)
-        coarse = []
-        for v in (1, 2, 3):
-            at = pl.ds((v * layers + layers - 1) * 2 * ca, 2 * ca)
-            tiles = obuf[at, :].reshape(ca // 8, 2, 8, LANES)
-            plane = jnp.concatenate([tiles[:, h].reshape(ca, LANES) for h in range(2)], axis=1)
-            across_mean = jnp.dot(
-                plane, halve, precision=lax.Precision.HIGHEST, preferred_element_type=F32
+        ).astype(BF16)
+
+        finish_halo()
+
+        layers = sections // 4
+        plane_row = lax.broadcasted_iota(jnp.int32, (ca, cb), 0)
+        plane_lane = lax.broadcasted_iota(jnp.int32, (ca, cb), 1)
+
+        def plane(k):
+            tiles = fbuf[pl.ds(k * 2 * ca, 2 * ca), :].reshape(ca // 8, 2, 8, LANES)
+            return jnp.concatenate([tiles[:, h].reshape(ca, LANES) for h in range(2)], axis=1)
+
+        def plane_lap(c, k):
+            up = jnp.where(plane_row == 0, tbuf[0, k : k + 1], pltpu.roll(c, 1, 0))
+            down = jnp.where(
+                plane_row == ca - 1, tbuf[ca + 1, k : k + 1], pltpu.roll(c, ca - 1, 0)
             )
-            coarse.append(
-                jnp.dot(
-                    halve_rows, across_mean, precision=lax.Precision.HIGHEST, preferred_element_type=F32
-                )
-            )
-        flux, quality, enthalpy = coarse
+            left = jnp.where(plane_lane == 0, 0.0, pltpu.roll(c, 1, 1))
+            right = jnp.where(plane_lane == cb - 1, 0.0, pltpu.roll(c, cb - 1, 1))
+            at = pl.ds(k * ca, ca)
+            halo_col = jnp.concatenate([hbuf[h, at] for h in range(2)], axis=1)
+            return up + down + (left + right + halo_col) - 4.0 * c
+
+        last = [v * layers + layers - 1 for v in range(4)]
+        d, m, q, e = (plane(k) for k in last)
+        if layers > 1:
+            dm, dq, de = (x - plane(k - 1) for x, k in zip((m, q, e), last[1:]))
+        else:
+            dm, dq, de = m, q, e
+        relaxing = relax_rate / (1.0 + d * d)
+        exits = [
+            m - cfl_nozzle * (dm + dq) + diffusion * plane_lap(m, last[1]),
+            q
+            + relax_step * relaxing * (e - q)
+            - cfl_nozzle * dq
+            + diffusion * plane_lap(q, last[2]),
+            e - cfl_nozzle * de + diffusion * plane_lap(e, last[3]),
+        ]
+        paired = jnp.concatenate([x + pltpu.roll(x, ca - 1, 0) for x in exits], axis=0)
+        hi = paired.astype(BF16)
+        rest = paired - hi.astype(F32)
+        mid, low = split_hi_lo(rest)
+        sums = jnp.dot(
+            jnp.concatenate([hi, mid, low], axis=0), halve, preferred_element_type=F32
+        )
+        coarse = sums[: 3 * ca] + sums[3 * ca : 6 * ca] + sums[6 * ca :]
+        flux, quality, enthalpy = (coarse[v * ca : (v + 1) * ca] for v in range(3))
         strength = jnp.sqrt(1.0 + flux * flux)
         center = (sections - 1) * jax.nn.sigmoid(enthalpy - 2.0 * quality)
         for base, value in ((0, strength), (2, center)):
-            hi, lo = split_hi_lo(value)
-            for k, part in ((base, hi.astype(F32)), (base + 1, lo.astype(F32))):
+            hi, low = split_hi_lo(value)
+            for k, part in ((base, hi.astype(F32)), (base + 1, low.astype(F32))):
                 for i in range(ca // 2):
-                    par[k : k + 1, i * (cb // 2) : (i + 1) * (cb // 2)] = part[i : i + 1]
-
-        group = 16
-        values = par[...]
+                    par[k : k + 1, i * (cb // 2) : (i + 1) * (cb // 2)] = part[2 * i : 2 * i + 1]
+
+        values = par[...].astype(BF16)
         tiled = jnp.concatenate([values] * group, axis=0)
-        label = jnp.right_shift(lax.broadcasted_iota(jnp.int32, (group * 8, exit_rows), 0), 3)
 
         @pl.loop(0, owners // group)
         def _(b):
-            picked = jnp.where(owner == label + b * group, tiled, 0.0).astype(BF16)
-            packed = dot_last(picked, in_slot).reshape(group, 8, SLOTS)
+            picked = tiled * picks[pl.ds(pl.multiple_of(b * group * 8, group * 8), group * 8)]
+            packed = dot_last(picked, in_slot[...]).reshape(group, 8, SLOTS)
             send_buf[pl.ds(b * group, group)] = jnp.concatenate(
                 [packed[:, :, :LANES], packed[:, :, LANES:]], axis=1
             ).astype(BF16)
@@ -326,6 +336,29 @@
                     device_id=(1, o // n_plane, o % n_plane),
                     device_id_type=MESH,
                 ).start()
+
+        @pl.loop(0, ca // CHUNK)
+        def _(step):
+            for t in range(CHUNK):
+                a = step * CHUNK + t
+                c, _, lap = neighbours(a)
+                back = jnp.where(jnp.bitwise_and(col_row, layers - 1) == 0, 0.0, pltpu.roll(c, 1, 0))
+                du = c - back
+                d, m, q, e = (c[v * layers : (v + 1) * layers] for v in range(4))
+                dm, dq, de = (du[v * layers : (v + 1) * layers] for v in (1, 2, 3))
+                relaxing = relax_rate / (1.0 + d * d)
+                fresh = diffusion * lap + jnp.concatenate(
+                    [
+                        d - cfl_nozzle * dm,
+                        m - cfl_nozzle * (dm + dq),
+                        q + relax_step * relaxing * (e - q) - cfl_nozzle * dq,
+                        e - cfl_nozzle * de,
+                    ],
+                    axis=0,
+                )
+                scatter_row(a, fresh)
+
+        store.start()
 
         @pl.loop(0, owners)
         def _(o):
@@ -450,6 +483,8 @@
             pltpu.VMEM((1, exit_rows), jnp.int32),
             pltpu.VMEM((1, exit_rows), jnp.int32),
             pltpu.VMEM((1, exit_rows), jnp.int32),
+            pltpu.VMEM((owners * 8, exit_rows), BF16),
+            pltpu.VMEM((SLOTS, exit_rows), BF16),
             pltpu.SemaphoreType.DMA,
             pltpu.SemaphoreType.DMA,
             pltpu.SemaphoreType.DMA((4,)),

time: 23.6 us -> 19.4 us (0.82)
  Pallas kernels: 21.1 us -> 16.9 us
    pallas_call x1, Pallas kernels: 21.1 us -> 16.9 us  [body(): pl.pallas_call(functools.partial(kernel, n_slab, n_plane, sections, ca, c...]
where the time goes in v2:
time: 19.4 us; the launch traced here: 19.2 us
  Pallas kernels  16.9 us (87%)
  local copies, waits for them, and re-layouts  2.31 us (12%)
    pallas_call x1, Pallas kernels, body(): pl.pallas_call(functools.partial(kernel, n_slab, n_plane, sections, ca, c...  16.9 us
    unnamed x1, local copies, waits for them, and re-layouts  2.31 us

profile of v2, /device:TPU:7, one launch (start us, length us, event | category | flops | bytes accessed | tf_op | source)
XLA Modules:
  0.0 19.2 jit_solution(5021877699736149520)
XLA Ops:
  0.0 16.9 %shard_map.82 = f32[2048,128]{1,0:T(8,128)} custom-call(f32[2048,128]{1,0:T(8,128)} %bitcast.11, f32[32]{0:T(128)} %evap_hbm.1, bf16[32,1024]{1,0:T(8,128)(2,1)} %coal_hbm.1, bf16[1024,640]{1,0:T(8,128)(2,1)} %constant.2.clone.fold_hbm, f32[8]{0:T(128)} %width_hbm.1, s32[1,2048]{1,0:T(1,128)} %owner_hbm.1, s32[1,2048]{1,0:T(1,128)} %cell_hbm.1, ...), custom_call_target="tpu_custom_call" | custom-call | tf_op jit(solution)/shard_map/pallas_call | solution.py:464
  16.9 2.3 %copy.10 = f32[1,32,32,256]{3,2,1,0:T(8,128)} copy(f32[1,32,32,256]{3,2,1,0:T(8,128)} %bitcast.10) | data formatting | bytes 2097152

commit v3 on v2

--- a/solution.py
+++ b/solution.py
@@ -69,29 +69,6 @@
     p = lax.axis_index("plane")
     me = s * n_plane + p
 
-    barrier = pltpu.get_barrier_semaphore()
-    sides = [
-        (s > 0, (g, s - 1, p)),
-        (s < n_slab - 1, (g, s + 1, p)),
-        (p > 0, (g, s, p - 1)),
-        (p < n_plane - 1, (g, s, p + 1)),
-    ]
-    near = 0
-    for there, target in sides:
-        near = near + there.astype(jnp.int32)
-
-        @pl.when(there)
-        def _():
-            pl.semaphore_signal(barrier, inc=1, device_id=target, device_id_type=MESH)
-
-    @pl.when(g == 1)
-    def _():
-        @pl.loop(0, owners)
-        def _(o):
-            pl.semaphore_signal(
-                barrier, inc=1, device_id=(0, o // n_plane, o % n_plane), device_id_type=MESH
-            )
-
     load = pltpu.make_async_copy(fields_hbm, fbuf, in_sem)
     load.start()
     nozzle_args = [
@@ -116,6 +93,29 @@
     def _():
         for copy in spray_args:
             copy.start()
+
+    barrier = pltpu.get_barrier_semaphore()
+    sides = [
+        (s > 0, (g, s - 1, p)),
+        (s < n_slab - 1, (g, s + 1, p)),
+        (p > 0, (g, s, p - 1)),
+        (p < n_plane - 1, (g, s, p + 1)),
+    ]
+    near = 0
+    for there, target in sides:
+        near = near + there.astype(jnp.int32)
+
+        @pl.when(there)
+        def _():
+            pl.semaphore_signal(barrier, inc=1, device_id=target, device_id_type=MESH)
+
+    @pl.when(g == 1)
+    def _():
+        @pl.loop(0, owners)
+        def _(o):
+            pl.semaphore_signal(
+                barrier, inc=1, device_id=(0, o // n_plane, o % n_plane), device_id_type=MESH
+            )
 
     load.wait()
 
@@ -451,6 +451,27 @@
         store.start()
 
     store.wait()
+
+
+def settle(held_hbm, out_hbm, buf, in_sem, out_sem):
+    pieces = in_sem.shape[0]
+    size = buf.shape[0] // pieces
+    parts = [pl.ds(k * size, size) for k in range(pieces)]
+    reads = [
+        pltpu.make_async_copy(held_hbm.at[at], buf.at[at], in_sem.at[k])
+        for k, at in enumerate(parts)
+    ]
+    writes = [
+        pltpu.make_async_copy(buf.at[at], out_hbm.at[at], out_sem.at[k])
+        for k, at in enumerate(parts)
+    ]
+    for read in reads:
+        read.start()
+    for read, write in zip(reads, writes):
+        read.wait()
+        write.start()
+    for write in writes:
+        write.wait()
 
 
 def body(n_slab, n_plane, fields, evap_rates, coal_kernel, plume_width, owner_map, deposit_cell, plume_ids):
@@ -500,6 +521,18 @@
         fields.reshape(rows // 8, 8, 2, LANES).transpose(0, 2, 1, 3).reshape(2 * rows, LANES), evap_rates, coal_kernel, fold, plume_width,
         owner_map, deposit_cell, plume_ids,
     )
+    out = pl.pallas_call(
+        settle,
+        out_shape=jax.ShapeDtypeStruct((2 * rows, LANES), F32),
+        in_specs=[hbm],
+        out_specs=hbm,
+        scratch_shapes=[
+            pltpu.VMEM((2 * rows, LANES), F32),
+            pltpu.SemaphoreType.DMA((4,)),
+            pltpu.SemaphoreType.DMA((4,)),
+        ],
+        compiler_params=pltpu.CompilerParams(vmem_limit_bytes=VMEM_BYTES),
+    )(out)
     out = out.reshape(rows // 8, 2, 8, LANES).transpose(0, 2, 1, 3)
     return out.reshape(1, sections, ca, cb)
 

time: 19.4 us -> 19 us (0.979)
  local copies, waits for them, and re-layouts: 2.31 us -> 0 us
  Pallas kernels: 16.9 us -> 18.7 us
    unnamed x1 -> x0, local copies, waits for them, and re-layouts: 2.31 us -> none
    pallas_call x0 -> x1, Pallas kernels: none -> 1.98 us  [body(): pl.pallas_call(settle, out_shape=jax.ShapeDtypeStruct((2 * rows, LANES),...]
where the time goes in v3:
time: 19 us; the launch traced here: 18.7 us
  Pallas kernels  18.7 us (98%)
    pallas_call x1, Pallas kernels, body(): pl.pallas_call(functools.partial(kernel, n_slab, n_plane, sections, ca, c...  16.7 us
    pallas_call x1, Pallas kernels, body(): pl.pallas_call(settle, out_shape=jax.ShapeDtypeStruct((2 * rows, LANES),...  1.98 us

profile of v3, /device:TPU:7, one launch (start us, length us, event | category | flops | bytes accessed | tf_op | source)
XLA Modules:
  0.0 18.7 jit_solution(13348552324152247992)
XLA Ops:
  0.0 16.7 %shard_map.82.held_hbm = f32[2048,128]{1,0:T(8,128)} custom-call(f32[2048,128]{1,0:T(8,128)} %bitcast.10, f32[32]{0:T(128)} %evap_hbm.1, bf16[32,1024]{1,0:T(8,128)(2,1)} %coal_hbm.1, bf16[1024,640]{1,0:T(8,128)(2,1)} %constant.2.clone.fold_hbm, f32[8]{0:T(128)} %width_hbm.1, s32[1,2048]{1,0:T(1,128)} %owner_hbm.1, s32[1,2048]{1,0:T(1,128)} %cell_hbm.1, ...), custom_call_target="tpu_custom_call" | custom-call | tf_op jit(solution)/shard_map/pallas_call | solution.py:485
  16.7 2.0 %shard_map.83 = f32[2048,128]{1,0:T(8,128)} custom-call(f32[2048,128]{1,0:T(8,128)} %shard_map.82.held_hbm), custom_call_target="tpu_custom_call" | custom-call | tf_op jit(solution)/shard_map/pallas_call | solution.py:524
